TPU v7x, 32 devices: a whole 2x2x4 slice. The times are simulated.
32 devices in a mesh: tm: 4 (over y, x), space: 8 (over z, core).
Axes of the slice: x: 2, y: 2, z: 4, core: 2. Of those that a mesh axis runs over, the one named last changes fastest.
Arguments:
- latent_clip: bfloat16 [8, 16, 32, 256], P('tm', 'space'), may hold values from -45 to 45
- cotangent: bfloat16 [8, 16, 32, 128], P('tm', 'space'), may hold values from -6 to 6
- conv_weight: bfloat16 [6912, 128], replicated, may hold values from -0.078125 to 0.078125
- norm_gain: float32 [256], replicated, may hold values from 0.5 to 1.5
- norm_shift: float32 [256], replicated, may hold values from -2 to 2
Outputs:
- clip_grad: bfloat16 [8, 16, 32, 256], P('tm', 'space')
- weight_grad: float32 [6912, 128], P('space')
- gain_grad: float32 [256], replicated
- shift_grad: float32 [256], replicated
All inputs are finite; a program needn't handle non-finite values.
Results may differ from a plain program's by a relative error of at most 0.0029.
Values may be sent and summed in bfloat16 or wider, within the bound.
A program may use at most 64 MiB of HBM per device.

v0:
```python
import jax
import jax.numpy as jnp
from jax import lax
from jax.sharding import PartitionSpec as P

GROUPS = 32


def shifted(value, axis, steps):
    count = lax.axis_size(axis)
    leading, last = (max(0, -steps), min(count, count - steps))
    return lax.ppermute(value, axis, [(source, source + steps) for source in range(leading, last)])


def extended_2(block, sides, width):
    for axis, dim in sides:
        count = lax.axis_size(axis)
        forward = [(i, i + 1) for i in range(count - 1)]
        backward = [(target, source) for source, target in forward]
        low = lax.ppermute(
            lax.slice_in_dim(block, block.shape[dim] - width, None, axis=dim), axis, forward
        )
        high = lax.ppermute(lax.slice_in_dim(block, 0, width, axis=dim), axis, backward)
        block = jnp.concatenate([low, block, high], axis=dim)
    return block


def silu_slope(activation):
    sigma = jax.nn.sigmoid(activation)
    return sigma * (1.0 + activation * (1.0 - sigma))


def tap_block(source, anchors, frame_count, row_count, col_count):
    pieces = [
        source[
            anchor[0] : anchor[0] + frame_count,
            anchor[1] : anchor[1] + row_count,
            anchor[2] : anchor[2] + col_count,
            :,
        ]
        for anchor in anchors
    ]
    merged = jnp.concatenate(pieces, axis=-1)
    return merged.reshape(frame_count * row_count * col_count, merged.shape[-1])


def transposed(grad_pad, conv_weight, frame_count, row_count, col_count):
    out_channels = conv_weight.shape[1]
    channels = conv_weight.shape[0] // 27
    kernel = conv_weight.reshape(3, 3, 3, channels, out_channels)
    total = jnp.zeros((frame_count * row_count * col_count, channels), jnp.float32)
    for tap_time in range(3):
        anchors = [
            (2 - tap_time, 2 - tap_row, 2 - tap_col) for tap_row in range(3) for tap_col in range(3)
        ]
        tap_cols = tap_block(grad_pad, anchors, frame_count, row_count, col_count)
        flipped = jnp.transpose(kernel[tap_time], (0, 1, 3, 2)).reshape(9 * out_channels, channels)
        total = total + jnp.dot(tap_cols, flipped, preferred_element_type=jnp.float32)
    return total.reshape(frame_count, row_count, col_count, channels)


def shards(latent_clip, cotangent, conv_weight, norm_gain, norm_shift):
    frame_count, row_count, col_count, channels = latent_clip.shape
    out_channels = cotangent.shape[-1]
    width_group = channels // GROUPS
    tm_size = lax.axis_size("tm")
    space_size = lax.axis_size("space")
    group_count = frame_count * row_count * col_count * width_group * tm_size * space_size
    values = latent_clip.astype(jnp.float32).reshape(
        frame_count, row_count, col_count, GROUPS, width_group
    )
    group_mean = lax.psum(jnp.sum(values, axis=(0, 1, 2, 4)), ("tm", "space")) / group_count
    centered = values - group_mean[:, None]
    group_var = (
        lax.psum(jnp.sum(centered * centered, axis=(0, 1, 2, 4)), ("tm", "space")) / group_count
    )
    inv_std = lax.rsqrt(group_var + 1e-06)
    normed = (centered * inv_std[:, None]).reshape(frame_count, row_count, col_count, channels)
    activation = normed * norm_gain + norm_shift
    hidden = jax.nn.silu(activation).astype(jnp.bfloat16)
    ahead = shifted(cotangent, "tm", -1)
    time_source = jnp.concatenate([cotangent, ahead], axis=0)
    time_pad = (0, 0)
    cached = shifted(hidden, "tm", 1)
    extended = jnp.concatenate([cached, hidden], axis=0)
    rimmed = extended_2(extended, (("space", 1),), 1)
    padded = jnp.pad(rimmed, ((0, 0), (0, 0), (1, 1), (0, 0)))
    cell_count = frame_count * row_count * col_count
    upstream = cotangent.reshape(cell_count, out_channels)
    tap_grads = []
    for tap_time in range(3):
        anchors = [(tap_time, tap_row, tap_col) for tap_row in range(3) for tap_col in range(3)]
        tap_cols = tap_block(padded, anchors, frame_count, row_count, col_count)
        tap_grads.append(
            lax.dot_general(
                tap_cols, upstream, (((0,), (0,)), ((), ())), preferred_element_type=jnp.float32
            )
        )
    local_grad = jnp.concatenate(tap_grads, axis=0)
    space_shard = lax.psum_scatter(local_grad, "space", scatter_dimension=0, tiled=True)
    weight_grad = lax.psum(space_shard, "tm")
    grad_pad = jnp.pad(time_source, (time_pad, (2, 2), (1, 1), (0, 0)))
    spread = transposed(grad_pad, conv_weight, frame_count, row_count + 2, col_count)
    from_below = shifted(spread[:, 0], "space", -1)
    from_above = shifted(spread[:, row_count + 1], "space", 1)
    inner = spread[:, 1 : row_count + 1]
    inner = inner.at[:, row_count - 1].add(from_below)
    inner = inner.at[:, 0].add(from_above)
    activation_grad = inner * silu_slope(activation)
    gain_grad, shift_grad = lax.psum(
        (
            jnp.sum(activation_grad * normed, axis=(0, 1, 2)),
            jnp.sum(activation_grad, axis=(0, 1, 2)),
        ),
        ("tm", "space"),
    )
    first = jnp.sum((norm_gain * shift_grad).reshape(GROUPS, width_group), axis=1)
    second = jnp.sum((norm_gain * gain_grad).reshape(GROUPS, width_group), axis=1)
    scaled = (activation_grad * norm_gain).reshape(
        frame_count, row_count, col_count, GROUPS, width_group
    )
    normed_groups = normed.reshape(frame_count, row_count, col_count, GROUPS, width_group)
    clip_grad = inv_std[:, None] * (
        scaled - first[:, None] / group_count - normed_groups * second[:, None] / group_count
    )
    clip_grad = clip_grad.reshape(frame_count, row_count, col_count, channels).astype(jnp.bfloat16)
    return (clip_grad, weight_grad, gain_grad, shift_grad)


def solution(mesh):
    return jax.shard_map(
        shards,
        mesh=mesh,
        in_specs=(P("tm", "space", None, None), P("tm", "space", None, None), P(), P(), P()),
        out_specs=(P("tm", "space", None, None), P("space", None), P(), P()),
        check_vma=False,
    )
```

profile of v0, /device:TPU:0, one launch (start us, length us, event | category | flops | bytes accessed | tf_op | source)
XLA Modules:
  0.0 225.5 jit_solution(13261450040164895884)
XLA Ops:
  7.2 0.9 convert_reduce_fusion
  8.3 1.3 collective-permute-start
  9.6 43.2 %psum.35 = f32[32]{0:T(128)S(1)} all-reduce(f32[32]{0:T(128)S(1)} %reduce_sum.70), channel_id=1, replica_groups=mesh['tm'=4,'space'=8] {'tm','space'}, use_global_device_ids=true, to_apply=%region_2.0 | all-reduce | flops 32 | bytes 256 | tf_op jit(solution)/shard_map/psum | solution.py:72
  52.9 0.9 fusion.33
  54.0 1.5 fusion.40
  55.6 41.0 %psum.36 = f32[32]{0:T(128)S(1)} all-reduce(f32[32]{0:T(128)S(1)} %reduce_sum.73), channel_id=1, replica_groups=mesh['tm'=4,'space'=8] {'tm','space'}, use_global_device_ids=true, to_apply=%region_5.6 | all-reduce | flops 32 | bytes 256 | tf_op jit(solution)/shard_map/psum | solution.py:75
  98.6 0.3 convolution_add_fusion.1
  99.4 1.3 collective-permute-start.1
  100.9 3.0 %collective-permute-start.2 = (f32[2,32,256]{2,1,0:T(8,128)S(1)}, f32[2,32,256]{2,1,0:T(8,128)S(1)}, u32[]{:S(2)}, u32[]{:S(2)}) collective-permute-start(f32[2,32,256]{2,1,0:T(8,128)S(1)} %get-tuple-element.53), channel_id=1, source_target_pairs={{0,1},{1,2},{2,3},{3,4},{4,5},{5,6},{6,7},{8,9},{9,10},{10,11},{11... | collective-permute-start | bytes 196616 | tf_op jit(solution)/shard_map/ppermute | solution.py:12
  103.9 0.9 collective-permute-done.2
  105.0 4.2 %collective-permute-start.3 = (bf16[2,2,32,256]{3,2,1,0:T(8,128)(2,1)S(1)}, bf16[2,2,32,256]{3,2,1,0:T(8,128)(2,1)S(1)}, u32[]{:S(2)}, u32[]{:S(2)}) collective-permute-start(bf16[2,2,32,256]{3,2,1,0:T(8,128)(2,1)S(1)} %get-tuple-element.90), channel_id=1, source_target_pairs={{0,8},{8,16},{16,24},{1,9},{9,17},{17,25},{2,10},{10,18},{18,26},{... | collective-permute-start | bytes 196616 | tf_op jit(solution)/shard_map/ppermute | solution.py:12
  109.1 1.9 collective-permute-done.3
  111.1 1.4 collective-permute-start.4
  112.6 1.3 collective-permute-start.5
  113.9 4.6 %collective-permute-done.5 = bf16[4,1,32,256]{3,2,1,0:T(8,128)(2,1)S(1)} collective-permute-done((bf16[4,1,32,256]{3,2,1,0:T(8,128)(2,1)S(1)}, bf16[4,1,32,256]{3,2,1,0:T(8,128)(2,1)S(1)}, u32[]{:S(2)}, u32[]{:S(2)}) %collective-permute-start.5) | collective-permute-done | bytes 65568 | tf_op jit(solution)/shard_map/ppermute | solution.py:23
  118.9 0.3 convolution_bitcast_fusion
  119.2 0.3 convolution_bitcast_fusion.2
  119.6 0.3 convolution_bitcast_fusion.1
  119.9 2.0 pad_maximum_fusion
  122.0 45.1 %all-reduce.2 = (f32[256]{0:T(256)S(1)}, f32[256]{0:T(256)S(1)}) all-reduce(f32[256]{0:T(256)S(1)} %get-tuple-element.29, f32[256]{0:T(256)S(1)} %get-tuple-element.28), channel_id=1, replica_groups=mesh['tm'=4,'space'=8] {'tm','space'}, use_global_device_ids=true, to_apply=%region_10.11 | all-reduce | flops 512 | bytes 4096 | tf_op jit(solution)/shard_map/psum | solution.py:110
  167.4 3.1 %reduce-scatter.2.cloned.1.call-done = f32[864,128]{1,0:T(8,128)} async-done(((f32[6912,128]{1,0:T(8,128)}), f32[864,128]{1,0:T(8,128)}) %reduce-scatter.2.cloned.1.call-update) | async-done | bytes 442384 | tf_op jit(solution)/shard_map/reduce_scatter | solution.py:100
  171.1 0.7 fusion.32
  171.8 45.1 %all-reduce.5.cloned.1.call-done = f32[864,128]{1,0:T(8,128)} async-done(((f32[864,128]{1,0:T(8,128)}), f32[864,128]{1,0:T(8,128)}) %all-reduce.5.cloned.1.call-update) | async-done | bytes 442384 | tf_op jit(solution)/shard_map/psum | solution.py:101
  216.9 1.8 copy.74
  (75 shorter events, 4.4 us)
Async XLA Ops:
  7.2 163.3 %reduce-scatter.2.cloned.1.call-start = ((), (), s32[]{:S(2)}) async-start(), calls=%async_computation.1 | async-start | bytes 3981312 | tf_op jit(solution)/shard_map/reduce_scatter | solution.py:100
  8.3 89.0 %collective-permute-start = (bf16[2,2,32,128]{3,2,1,0:T(8,128)(2,1)}, bf16[2,2,32,128]{3,2,1,0:T(8,128)(2,1)S(1)}, u32[]{:S(2)}, u32[]{:S(2)}) collective-permute-start(bf16[2,2,32,128]{3,2,1,0:T(8,128)(2,1)} %param.10), channel_id=1, source_target_pairs={{8,0},{16,8},{24,16},{9,1},{17,9},{25,17},{10,2},{18,10},{26,18},{... | collective-permute-start | bytes 98312 | tf_op jit(solution)/shard_map/ppermute | solution.py:12
  96.8 0.8 copy-start.1
  99.0 5.8 %copy-start = (bf16[2,2,32,256]{3,2,1,0:T(8,128)(2,1)S(1)}, bf16[2,2,32,256]{3,2,1,0:T(8,128)(2,1)}, u32[]{:S(2)}) copy-start(bf16[2,2,32,256]{3,2,1,0:T(8,128)(2,1)} %param.9) | copy-start | bytes 196612
  99.0 5.8 %copy-start.2 = (f32[256]{0:T(256)S(1)}, f32[256]{0:T(256)}, u32[]{:S(2)}) copy-start(f32[256]{0:T(256)} %param.12) | copy-start | bytes 3076
  99.0 5.8 %copy-start.3 = (f32[256]{0:T(256)S(1)}, f32[256]{0:T(256)}, u32[]{:S(2)}) copy-start(f32[256]{0:T(256)} %param.13) | copy-start | bytes 3076
  99.4 4.5 %collective-permute-start.1 = (f32[2,32,256]{2,1,0:T(8,128)S(1)}, f32[2,32,256]{2,1,0:T(8,128)S(1)}, u32[]{:S(2)}, u32[]{:S(2)}) collective-permute-start(f32[2,32,256]{2,1,0:T(8,128)S(1)} %get-tuple-element.54), channel_id=1, source_target_pairs={{1,0},{2,1},{3,2},{4,3},{5,4},{6,5},{7,6},{9,8},{10,9},{11,10},{12... | collective-permute-start | bytes 196616 | tf_op jit(solution)/shard_map/ppermute | solution.py:12
  100.9 3.9 %collective-permute-start.2 = (f32[2,32,256]{2,1,0:T(8,128)S(1)}, f32[2,32,256]{2,1,0:T(8,128)S(1)}, u32[]{:S(2)}, u32[]{:S(2)}) collective-permute-start(f32[2,32,256]{2,1,0:T(8,128)S(1)} %get-tuple-element.53), channel_id=1, source_target_pairs={{0,1},{1,2},{2,3},{3,4},{4,5},{5,6},{6,7},{8,9},{9,10},{10,11},{11... | collective-permute-start | bytes 196616 | tf_op jit(solution)/shard_map/ppermute | solution.py:12
  105.0 6.1 %collective-permute-start.3 = (bf16[2,2,32,256]{3,2,1,0:T(8,128)(2,1)S(1)}, bf16[2,2,32,256]{3,2,1,0:T(8,128)(2,1)S(1)}, u32[]{:S(2)}, u32[]{:S(2)}) collective-permute-start(bf16[2,2,32,256]{3,2,1,0:T(8,128)(2,1)S(1)} %get-tuple-element.90), channel_id=1, source_target_pairs={{0,8},{8,16},{16,24},{1,9},{9,17},{17,25},{2,10},{10,18},{18,26},{... | collective-permute-start | bytes 196616 | tf_op jit(solution)/shard_map/ppermute | solution.py:12
  111.1 2.8 %collective-permute-start.4 = (bf16[4,1,32,256]{3,2,1,0:T(8,128)(2,1)S(1)}, bf16[4,1,32,256]{3,2,1,0:T(8,128)(2,1)S(1)}, u32[]{:S(2)}, u32[]{:S(2)}) collective-permute-start(bf16[4,1,32,256]{3,2,1,0:T(8,128)(2,1)S(1)} %get-tuple-element.88), channel_id=1, source_target_pairs={{0,1},{1,2},{2,3},{3,4},{4,5},{5,6},{6,7},{8,9},{9,10},{10,11},{11... | collective-permute-start | bytes 196616 | tf_op jit(solution)/shard_map/ppermute | solution.py:20
  112.6 5.9 %collective-permute-start.5 = (bf16[4,1,32,256]{3,2,1,0:T(8,128)(2,1)S(1)}, bf16[4,1,32,256]{3,2,1,0:T(8,128)(2,1)S(1)}, u32[]{:S(2)}, u32[]{:S(2)}) collective-permute-start(bf16[4,1,32,256]{3,2,1,0:T(8,128)(2,1)S(1)} %get-tuple-element.89), channel_id=1, source_target_pairs={{1,0},{2,1},{3,2},{4,3},{5,4},{6,5},{7,6},{9,8},{10,9},{11,10},{12... | collective-permute-start | bytes 196616 | tf_op jit(solution)/shard_map/ppermute | solution.py:23
  122.0 94.9 %all-reduce.5.cloned.1.call-start = ((), (), s32[]{:S(2)}) async-start(), calls=%async_computation.2 | async-start | bytes 884736 | tf_op jit(solution)/shard_map/psum | solution.py:101
  167.2 51.5 %copy-start.4 = (f32[256]{0:T(256)}, f32[256]{0:T(256)S(1)}, u32[]{:S(2)}) copy-start(f32[256]{0:T(256)S(1)} %get-tuple-element.97) | copy-start | bytes 3076
  167.2 51.5 %copy-start.5 = (f32[256]{0:T(256)}, f32[256]{0:T(256)S(1)}, u32[]{:S(2)}) copy-start(f32[256]{0:T(256)S(1)} %get-tuple-element.98) | copy-start | bytes 3076
Sparse Core Ops, SparseCore 0:
  122.1 48.3 reduce-scatter.1
  173.8 43.0 all-reduce.4
where the time goes:
time: 226 us
  blocking collectives  129 us (57%)
  waiting for transfers between devices  55.6 us (25%)
  between operations  14.5 us (6%)
  starting transfers between devices  12.6 us (6%)
  local copies, waits for them, and re-layouts  6.15 us (3%)
  other arithmetic  5.25 us (2%)
    psum x1, blocking collectives, shards(): lax.psum((jnp.sum(activation_grad * normed, axis=(0, 1, 2)), jnp.sum(acti...  45.1 us
    psum x1, waiting for transfers between devices, shards(): weight_grad = lax.psum(space_shard, 'tm')  45.1 us
    psum x1, blocking collectives, shards(): lax.psum(jnp.sum(values, axis=(0, 1, 2, 4)), ('tm', 'space')) / group_count  43.2 us
    psum x1, blocking collectives, shards(): lax.psum(jnp.sum(centered * centered, axis=(0, 1, 2, 4)), ('tm', 'space'))  41 us
    ppermute x4, starting transfers between devices, shifted(): lax.ppermute(value, axis, [(source, source + steps) for source in range(l...  9.8 us
    ppermute x1, waiting for transfers between devices, extended_2(): lax.ppermute(lax.slice_in_dim(block, 0, width, axis=dim), axis, backward)  4.55 us
  transfers between devices with their start and end apart: 8, of which 5 were waited for; matrix products, arithmetic and copies ran while one was open for 2% of the time, Pallas kernels for 0%

commit v1 on v0

--- a/solution.py
+++ b/solution.py
@@ -98,7 +98,11 @@
         )
     local_grad = jnp.concatenate(tap_grads, axis=0)
     space_shard = lax.psum_scatter(local_grad, "space", scatter_dimension=0, tiled=True)
-    weight_grad = lax.psum(space_shard, "tm")
+    weight_grad = space_shard
+    for hop in (1, 2):
+        weight_grad = weight_grad + lax.ppermute(
+            weight_grad, "tm", [(dev, dev ^ hop) for dev in range(4)]
+        )
     grad_pad = jnp.pad(time_source, (time_pad, (2, 2), (1, 1), (0, 0)))
     spread = transposed(grad_pad, conv_weight, frame_count, row_count + 2, col_count)
     from_below = shifted(spread[:, 0], "space", -1)

time: 226 us -> 235 us (1.040)
  waiting for transfers between devices: 55.6 us -> 62.4 us
  starting transfers between devices: 12.6 us -> 16.4 us
    psum x1 -> x0, waiting for transfers between devices: 45.1 us -> none  [shards(): weight_grad = lax.psum(space_shard, 'tm')]
    reduce_scatter x1, waiting for transfers between devices: 3.13 us -> 47.5 us  [shards(): lax.psum_scatter(local_grad, 'space', scatter_dimension=0, tiled=True)]
    ppermute x0 -> x2, waiting for transfers between devices: none -> 7.6 us  [shards(): lax.ppermute(weight_grad, 'tm', [(dev, dev ^ hop) for dev in range(4)])]
    ppermute x0 -> x2, starting transfers between devices: none -> 3.83 us  [shards(): lax.ppermute(weight_grad, 'tm', [(dev, dev ^ hop) for dev in range(4)])]
  transfers between devices with their start and end apart: 8 -> 9, of which waited for: 5 -> 5; matrix products, arithmetic and copies ran while one was open for 2% -> 2% of each run, Pallas kernels for 0% -> 0%
where the time goes in v1:
time: 235 us; the launch traced here: 234 us
  blocking collectives  127 us (54%)
  waiting for transfers between devices  62.4 us (27%)
  starting transfers between devices  16.4 us (7%)
  between operations  14.5 us (6%)
  other arithmetic  7.11 us (3%)
  local copies, waits for them, and re-layouts  4.35 us (2%)
    reduce_scatter x1, waiting for transfers between devices, shards(): lax.psum_scatter(local_grad, 'space', scatter_dimension=0, tiled=True)  47.5 us
    psum x1, blocking collectives, shards(): lax.psum(jnp.sum(values, axis=(0, 1, 2, 4)), ('tm', 'space')) / group_count  43.2 us
    psum x1, blocking collectives, shards(): lax.psum((jnp.sum(activation_grad * normed, axis=(0, 1, 2)), jnp.sum(acti...  43 us
    psum x1, blocking collectives, shards(): lax.psum(jnp.sum(centered * centered, axis=(0, 1, 2, 4)), ('tm', 'space'))  41 us
    ppermute x4, starting transfers between devices, shifted(): lax.ppermute(value, axis, [(source, source + steps) for source in range(l...  9.8 us
    ppermute x2, waiting for transfers between devices, shards(): lax.ppermute(weight_grad, 'tm', [(dev, dev ^ hop) for dev in range(4)])  7.6 us
  transfers between devices with their start and end apart: 9, of which 5 were waited for; matrix products, arithmetic and copies ran while one was open for 2% of the time, Pallas kernels for 0%

profile of v1, /device:TPU:0, one launch (start us, length us, event | category | flops | bytes accessed | tf_op | source)
XLA Modules:
  0.0 234.0 jit_solution(17456278367312747065)
XLA Ops:
  7.2 0.9 convert_reduce_fusion
  8.3 1.3 collective-permute-start
  9.6 43.2 %psum.28 = f32[32]{0:T(128)S(1)} all-reduce(f32[32]{0:T(128)S(1)} %reduce_sum.70), channel_id=1, replica_groups=mesh['tm'=4,'space'=8] {'tm','space'}, use_global_device_ids=true, to_apply=%region_2.0 | all-reduce | flops 32 | bytes 256 | tf_op jit(solution)/shard_map/psum | solution.py:72
  52.9 0.9 fusion.33
  54.0 1.5 fusion.40
  55.6 41.0 %psum.29 = f32[32]{0:T(128)S(1)} all-reduce(f32[32]{0:T(128)S(1)} %reduce_sum.73), channel_id=1, replica_groups=mesh['tm'=4,'space'=8] {'tm','space'}, use_global_device_ids=true, to_apply=%region_5.6 | all-reduce | flops 32 | bytes 256 | tf_op jit(solution)/shard_map/psum | solution.py:75
  99.0 0.3 convolution_add_fusion
  99.4 1.3 collective-permute-start.1
  100.9 3.0 %collective-permute-start.2 = (f32[2,32,256]{2,1,0:T(8,128)S(1)}, f32[2,32,256]{2,1,0:T(8,128)S(1)}, u32[]{:S(2)}, u32[]{:S(2)}) collective-permute-start(f32[2,32,256]{2,1,0:T(8,128)S(1)} %get-tuple-element.53), channel_id=1, source_target_pairs={{0,1},{1,2},{2,3},{3,4},{4,5},{5,6},{6,7},{8,9},{9,10},{10,11},{11... | collective-permute-start | bytes 196616 | tf_op jit(solution)/shard_map/ppermute | solution.py:12
  104.0 0.9 collective-permute-done.2
  105.0 4.2 %collective-permute-start.3 = (bf16[2,2,32,256]{3,2,1,0:T(8,128)(2,1)S(1)}, bf16[2,2,32,256]{3,2,1,0:T(8,128)(2,1)S(1)}, u32[]{:S(2)}, u32[]{:S(2)}) collective-permute-start(bf16[2,2,32,256]{3,2,1,0:T(8,128)(2,1)S(1)} %get-tuple-element.90), channel_id=1, source_target_pairs={{0,8},{8,16},{16,24},{1,9},{9,17},{17,25},{2,10},{10,18},{18,26},{... | collective-permute-start | bytes 196616 | tf_op jit(solution)/shard_map/ppermute | solution.py:12
  109.2 1.9 collective-permute-done.3
  111.1 1.4 collective-permute-start.4
  112.6 1.3 collective-permute-start.5
  113.9 4.6 %collective-permute-done.5 = bf16[4,1,32,256]{3,2,1,0:T(8,128)(2,1)S(1)} collective-permute-done((bf16[4,1,32,256]{3,2,1,0:T(8,128)(2,1)S(1)}, bf16[4,1,32,256]{3,2,1,0:T(8,128)(2,1)S(1)}, u32[]{:S(2)}, u32[]{:S(2)}) %collective-permute-start.5) | collective-permute-done | bytes 65568 | tf_op jit(solution)/shard_map/ppermute | solution.py:23
  120.0 2.0 pad_maximum_fusion
  122.0 47.5 %reduce-scatter.2.cloned.1.call-done = f32[864,128]{1,0:T(8,128)} async-done(((f32[6912,128]{1,0:T(8,128)}), f32[864,128]{1,0:T(8,128)}) %reduce-scatter.2.cloned.1.call-update) | async-done | bytes 442384 | tf_op jit(solution)/shard_map/reduce_scatter | solution.py:100
  169.4 1.5 collective-permute-start.6
  170.9 43.0 %all-reduce.2 = (f32[256]{0:T(256)S(1)}, f32[256]{0:T(256)S(1)}) all-reduce(f32[256]{0:T(256)S(1)} %get-tuple-element.29, f32[256]{0:T(256)S(1)} %get-tuple-element.28), channel_id=1, replica_groups=mesh['tm'=4,'space'=8] {'tm','space'}, use_global_device_ids=true, to_apply=%region_10.11 | all-reduce | flops 512 | bytes 4096 | tf_op jit(solution)/shard_map/psum | solution.py:114
  214.1 1.1 add.72
  215.2 2.3 collective-permute-start.7
  218.1 0.7 fusion.32
  218.8 7.6 %collective-permute-done.7 = f32[864,128]{1,0:T(8,128)S(1)} collective-permute-done((f32[864,128]{1,0:T(8,128)S(1)}, f32[864,128]{1,0:T(8,128)S(1)}, u32[]{:S(2)}, u32[]{:S(2)}) %collective-permute-start.7) | collective-permute-done | bytes 442400 | tf_op jit(solution)/shard_map/ppermute | solution.py:103
  226.4 0.8 add.73
  (77 shorter events, 5.4 us)
Async XLA Ops:
  7.2 162.3 %reduce-scatter.2.cloned.1.call-start = ((), (), s32[]{:S(2)}) async-start(), calls=%async_computation.1 | async-start | bytes 3981312 | tf_op jit(solution)/shard_map/reduce_scatter | solution.py:100
  8.3 89.1 %collective-permute-start = (bf16[2,2,32,128]{3,2,1,0:T(8,128)(2,1)}, bf16[2,2,32,128]{3,2,1,0:T(8,128)(2,1)S(1)}, u32[]{:S(2)}, u32[]{:S(2)}) collective-permute-start(bf16[2,2,32,128]{3,2,1,0:T(8,128)(2,1)} %param.10), channel_id=1, source_target_pairs={{8,0},{16,8},{24,16},{9,1},{17,9},{25,17},{10,2},{18,10},{26,18},{... | collective-permute-start | bytes 98312 | tf_op jit(solution)/shard_map/ppermute | solution.py:12
  96.8 0.8 copy-start.1
  99.0 5.9 %copy-start = (bf16[2,2,32,256]{3,2,1,0:T(8,128)(2,1)S(1)}, bf16[2,2,32,256]{3,2,1,0:T(8,128)(2,1)}, u32[]{:S(2)}) copy-start(bf16[2,2,32,256]{3,2,1,0:T(8,128)(2,1)} %param.9) | copy-start | bytes 196612
  99.0 5.8 %copy-start.2 = (f32[256]{0:T(256)S(1)}, f32[256]{0:T(256)}, u32[]{:S(2)}) copy-start(f32[256]{0:T(256)} %param.12) | copy-start | bytes 3076
  99.0 5.8 %copy-start.3 = (f32[256]{0:T(256)S(1)}, f32[256]{0:T(256)}, u32[]{:S(2)}) copy-start(f32[256]{0:T(256)} %param.13) | copy-start | bytes 3076
  99.4 4.5 %collective-permute-start.1 = (f32[2,32,256]{2,1,0:T(8,128)S(1)}, f32[2,32,256]{2,1,0:T(8,128)S(1)}, u32[]{:S(2)}, u32[]{:S(2)}) collective-permute-start(f32[2,32,256]{2,1,0:T(8,128)S(1)} %get-tuple-element.54), channel_id=1, source_target_pairs={{1,0},{2,1},{3,2},{4,3},{5,4},{6,5},{7,6},{9,8},{10,9},{11,10},{12... | collective-permute-start | bytes 196616 | tf_op jit(solution)/shard_map/ppermute | solution.py:12
  100.9 3.9 %collective-permute-start.2 = (f32[2,32,256]{2,1,0:T(8,128)S(1)}, f32[2,32,256]{2,1,0:T(8,128)S(1)}, u32[]{:S(2)}, u32[]{:S(2)}) collective-permute-start(f32[2,32,256]{2,1,0:T(8,128)S(1)} %get-tuple-element.53), channel_id=1, source_target_pairs={{0,1},{1,2},{2,3},{3,4},{4,5},{5,6},{6,7},{8,9},{9,10},{10,11},{11... | collective-permute-start | bytes 196616 | tf_op jit(solution)/shard_map/ppermute | solution.py:12
  105.0 6.1 %collective-permute-start.3 = (bf16[2,2,32,256]{3,2,1,0:T(8,128)(2,1)S(1)}, bf16[2,2,32,256]{3,2,1,0:T(8,128)(2,1)S(1)}, u32[]{:S(2)}, u32[]{:S(2)}) collective-permute-start(bf16[2,2,32,256]{3,2,1,0:T(8,128)(2,1)S(1)} %get-tuple-element.90), channel_id=1, source_target_pairs={{0,8},{8,16},{16,24},{1,9},{9,17},{17,25},{2,10},{10,18},{18,26},{... | collective-permute-start | bytes 196616 | tf_op jit(solution)/shard_map/ppermute | solution.py:12
  111.1 2.8 %collective-permute-start.4 = (bf16[4,1,32,256]{3,2,1,0:T(8,128)(2,1)S(1)}, bf16[4,1,32,256]{3,2,1,0:T(8,128)(2,1)S(1)}, u32[]{:S(2)}, u32[]{:S(2)}) collective-permute-start(bf16[4,1,32,256]{3,2,1,0:T(8,128)(2,1)S(1)} %get-tuple-element.88), channel_id=1, source_target_pairs={{0,1},{1,2},{2,3},{3,4},{4,5},{5,6},{6,7},{8,9},{9,10},{10,11},{11... | collective-permute-start | bytes 196616 | tf_op jit(solution)/shard_map/ppermute | solution.py:20
  112.6 5.9 %collective-permute-start.5 = (bf16[4,1,32,256]{3,2,1,0:T(8,128)(2,1)S(1)}, bf16[4,1,32,256]{3,2,1,0:T(8,128)(2,1)S(1)}, u32[]{:S(2)}, u32[]{:S(2)}) collective-permute-start(bf16[4,1,32,256]{3,2,1,0:T(8,128)(2,1)S(1)} %get-tuple-element.89), channel_id=1, source_target_pairs={{1,0},{2,1},{3,2},{4,3},{5,4},{6,5},{7,6},{9,8},{10,9},{11,10},{12... | collective-permute-start | bytes 196616 | tf_op jit(solution)/shard_map/ppermute | solution.py:23
  169.4 44.7 %collective-permute-start.6 = (f32[864,128]{1,0:T(8,128)}, f32[864,128]{1,0:T(8,128)S(1)}, u32[]{:S(2)}, u32[]{:S(2)}) collective-permute-start(f32[864,128]{1,0:T(8,128)} %reduce-scatter.2.cloned.1.call-done), channel_id=1, source_target_pairs={{0,8},{8,0},{16,24},{24,16},{1,9},{9,1},{17,25},{25,17},{2,10},{10... | collective-permute-start | bytes 1327112 | tf_op jit(solution)/shard_map/ppermute | solution.py:103
  213.9 13.3 %copy-start.4 = (f32[256]{0:T(256)}, f32[256]{0:T(256)S(1)}, u32[]{:S(2)}) copy-start(f32[256]{0:T(256)S(1)} %get-tuple-element.30) | copy-start | bytes 3076
  213.9 13.3 %copy-start.5 = (f32[256]{0:T(256)}, f32[256]{0:T(256)S(1)}, u32[]{:S(2)}) copy-start(f32[256]{0:T(256)S(1)} %get-tuple-element.31) | copy-start | bytes 3076
  215.2 11.2 %collective-permute-start.7 = (f32[864,128]{1,0:T(8,128)S(1)}, f32[864,128]{1,0:T(8,128)S(1)}, u32[]{:S(2)}, u32[]{:S(2)}) collective-permute-start(f32[864,128]{1,0:T(8,128)S(1)} %add.72), channel_id=1, source_target_pairs={{0,16},{8,24},{16,0},{24,8},{1,17},{9,25},{17,1},{25,9},{2,18},{10... | collective-permute-start | bytes 1327112 | tf_op jit(solution)/shard_map/ppermute | solution.py:103
Sparse Core Ops, SparseCore 0:
  122.1 47.3 reduce-scatter.1
